TPU v7x, 32 devices: a whole 2x2x4 slice. The times are simulated.
32 devices in a mesh: region: 8 (over z, y), member: 4 (over x, core).
Axes of the slice: x: 2, y: 2, z: 4, core: 2. Of those that a mesh axis runs over, the one named last changes fastest.
Arguments:
- control: float32 [64, 4, 128, 512], P('member', None, 'region'), may hold values from -6 to 6
- members: bfloat16 [64, 3, 4, 128, 512], P('member', None, None, 'region'), may hold values from -0.75 to 0.75
- obs_tile: int32 [4096, 1], P('region'), may hold values from 0 to 7; in each aligned block of 512 rows (0 to 511, 512 to 1023, ...) at most 256 rows name the same one
- obs_cell: int32 [4096], P('region'), may hold values from 0 to 98303
- innovation: float32 [4096], P('region'), may hold values from -6 to 6
- obs_weight: float32 [4096], P('region'), may hold values from 1 to 20
Outputs:
- gradient: float32 [64, 4, 128, 512], P('member', None, 'region')
Inputs may be any that keep to these rules, and one draw needn't show every extreme that they name: `obs_tile`: among the 512 observations of each device's block, at most 256 name the same tile; in every draw some tile is named by exactly 256 of some block. Tiles receive unequal numbers of observations.
All inputs are finite; a program needn't handle non-finite values.
Results may differ from a plain program's by a relative error of at most 0.0003.
Values may be sent and summed in bfloat16 or wider, within the bound.
A program may use at most 128 MiB of HBM per device.

v0:
```python
import jax
import jax.numpy as jnp
from jax import lax
from jax.sharding import PartitionSpec as P

HALF = 15


def extended(array, sides, width):
    for axis, dim in sides:
        count, length = (lax.axis_size(axis), array.shape[dim])
        up = [(i, (i + 1) % count) for i in range(count)]
        down = [(j, i) for i, j in up]
        last = lax.slice_in_dim(array, length - width, length, axis=dim)
        first = lax.slice_in_dim(array, 0, width, axis=dim)
        before = lax.ppermute(last, axis, up)
        after = lax.ppermute(first, axis, down)
        array = jnp.concatenate([before, array, after], axis=dim)
    return array


def tap_weight(dist):
    span = jnp.arange(-HALF, HALF + 1).astype(jnp.float32)
    total = jnp.sqrt(jnp.sum(jnp.exp(-span * span / 36.0)))
    return jnp.exp(-dist * dist / 72.0) / total


def band_table(count_rows, count_cols, offset):
    rows = jnp.arange(count_rows)[:, None]
    cols = jnp.arange(count_cols)[None, :]
    step = cols - rows - offset
    dist = step.astype(jnp.float32)
    return jnp.where(jnp.abs(step) <= HALF, tap_weight(dist), 0.0)


def field_pad(field):
    return extended(field, (("region", 2),), HALF)


def local(control, members, obs_tile, obs_cell, innovation, obs_weight):
    width_x = control.shape[2]
    width_y = control.shape[3]
    across_table = band_table(width_x, width_x + 2 * HALF, HALF)
    down_table = band_table(width_y, width_y, 0)

    def smooth(padded):
        across = jnp.einsum(
            "ij,...jy->...iy", across_table, padded, precision=lax.Precision.HIGHEST
        )
        return jnp.einsum("...iy,yz->...iz", across, down_table, precision=lax.Precision.HIGHEST)

    regions = lax.axis_size("region")
    obs_dev = obs_cell.shape[0]
    capacity = 4 * obs_dev // regions
    owner = obs_tile[:, 0]
    onehot = (owner[:, None] == jnp.arange(regions)[None, :]).astype(jnp.int32)
    ranks = jnp.sum(jnp.cumsum(onehot, axis=0) * onehot, axis=1) - 1
    slots = owner * capacity + ranks
    requests = (
        jnp.full((regions * capacity,), -1, jnp.int32)
        .at[slots]
        .set(obs_cell)
        .reshape(regions, capacity)
    )
    innov_buf = (
        jnp.zeros((regions * capacity,), jnp.float32)
        .at[slots]
        .set(innovation)
        .reshape(regions, capacity)
    )
    weight_buf = (
        jnp.zeros((regions * capacity,), jnp.float32)
        .at[slots]
        .set(obs_weight)
        .reshape(regions, capacity)
    )
    cells_in = lax.all_to_all(requests, "region", split_axis=0, concat_axis=0, tiled=True)
    innov_in, weight_in = (
        lax.all_to_all(innov_buf, "region", split_axis=0, concat_axis=0, tiled=True),
        lax.all_to_all(weight_buf, "region", split_axis=0, concat_axis=0, tiled=True),
    )
    spread = smooth(field_pad(control))
    partial_sum = jnp.sum(members * spread[:, None], axis=0)
    live = cells_in >= 0
    index_in = jnp.maximum(cells_in, 0)
    sampled = partial_sum.reshape(-1)[index_in]
    modelled = lax.psum(sampled, "member")
    weighted = jnp.where(live, weight_in * (modelled - innov_in), 0.0)
    flat_index = index_in.reshape(-1)
    flat_weighted = weighted.reshape(-1)
    adjoint = (
        jnp.zeros((partial_sum.size,), jnp.float32)
        .at[flat_index]
        .add(flat_weighted)
        .reshape(partial_sum.shape)
    )
    back = jnp.sum(members * adjoint[None], axis=1)
    back_pad = field_pad(back)
    return control + smooth(back_pad)


def solution(mesh):
    placed = (
        P("member", None, "region", None),
        P("member", None, None, "region", None),
        P("region", None),
        P("region"),
        P("region"),
        P("region"),
    )
    return jax.shard_map(
        local,
        mesh=mesh,
        in_specs=placed,
        out_specs=P("member", None, "region", None),
        check_vma=False,
    )
```

profile of v0, /device:TPU:0, one launch (start us, length us, event | category | flops | bytes accessed | tf_op | source)
XLA Modules:
  0.0 274.4 jit_solution(6770016381614072577)
XLA Ops:
  0.0 2.8 %fusion.86 = (f32[16,4,15,512]{3,2,1,0:T(8,128)S(1)}, f32[16,4,15,512]{3,2,1,0:T(8,128)S(1)}) fusion(f32[16,4,16,512]{3,2,1,0:T(8,128)} %param.6), kind=kLoop, calls=%fused_computation.101 | loop fusion | bytes 7864320 | tf_op jit(solution)/shard_map/slice | solution.py:14
  4.0 6.1 %collective-permute-start.1 = (f32[16,4,15,512]{3,0,2,1:T(8,128)S(1)}, f32[16,4,15,512]{3,0,2,1:T(8,128)}, u32[]{:S(2)}, u32[]{:S(2)}) collective-permute-start(f32[16,4,15,512]{3,0,2,1:T(8,128)S(1)} %copy.22), channel_id=1, source_target_pairs={{4,0},{8,4},{12,8},{16,12},{20,16},{24,20},{28,24},{0,28},{5,1},{9... | collective-permute-start | bytes 5898248 | tf_op jit(solution)/shard_map/ppermute | solution.py:17
  10.0 2.4 copy.21
  14.0 3.2 %scatter_custom_fusion = s32[2048]{0:T(1024)} fusion(s32[512]{0:T(512)S(1)} %bitcast.65, s32[512]{0:T(512)} %param.9, s32[]{:T(128)} %constant.11.clone.1), kind=kCustom, calls=%fused_computation.77 | custom fusion | bytes 8704 | tf_op jit(solution)/shard_map/scatter | solution.py:62
  17.1 6.0 %all-to-all-start = ((s32[8,1,256]{2,1,0:T(1,128)}), s32[8,1,256]{2,1,0:T(1,128)S(1)}, u32[]{:S(2)}, u32[]{:S(2)}) async-start(s32[8,1,256]{2,1,0:T(1,128)} %bitcast.6), calls=%async_computation | async-start | bytes 16384 | tf_op jit(solution)/shard_map/all_to_all | solution.py:77
  24.5 3.2 %scatter_custom_fusion.2 = f32[2048]{0:T(1024)} fusion(s32[512]{0:T(512)S(1)} %bitcast.66, f32[512]{0:T(512)} %param.10, f32[]{:T(128)} %constant.10.clone.1), kind=kCustom, calls=%fused_computation.73 | custom fusion | bytes 8704 | tf_op jit(solution)/shard_map/scatter | solution.py:68
  27.6 3.2 %scatter_custom_fusion.1 = f32[2048]{0:T(1024)} fusion(s32[512]{0:T(512)S(1)} %bitcast.67, f32[512]{0:T(512)} %param.11, f32[]{:T(128)} %constant.10.clone.1), kind=kCustom, calls=%fused_computation.75 | custom fusion | bytes 8704 | tf_op jit(solution)/shard_map/scatter | solution.py:74
  30.8 61.5 %all-to-all-done = s32[8,1,256]{2,1,0:T(1,128)S(1)} async-done(((s32[8,1,256]{2,1,0:T(1,128)}), s32[8,1,256]{2,1,0:T(1,128)S(1)}, u32[]{:S(2)}, u32[]{:S(2)}) %all-to-all-start) | async-done | bytes 8224 | tf_op jit(solution)/shard_map/all_to_all | solution.py:77
  92.3 8.9 %all-to-all-start.1 = ((f32[8,1,256]{2,1,0:T(1,128)}), f32[8,1,256]{2,1,0:T(1,128)S(1)}, u32[]{:S(2)}, u32[]{:S(2)}) async-start(f32[8,1,256]{2,1,0:T(1,128)} %bitcast.8), calls=%async_computation.1 | async-start | bytes 16384 | tf_op jit(solution)/shard_map/all_to_all | solution.py:80
  101.2 2.7 copy.12
  103.9 2.8 %copy.11 = f32[16,4,15,512]{3,2,1,0:T(8,128)S(1)} copy(f32[16,4,15,512]{3,0,2,1:T(8,128)} %collective-permute-done) | data formatting | bytes 3932160 | tf_op jit(solution)/shard_map/ppermute | solution.py:16
  106.8 6.2 %fusion.2 = f32[16,4,512,16]{2,3,1,0:T(8,128)S(1)} fusion(f32[16,4,15,512]{3,2,1,0:T(8,128)S(1)} %copy.12, f32[16,4,16,512]{3,2,1,0:T(8,128)S(1)} %copy-done, f32[16,4,15,512]{3,2,1,0:T(8,128)S(1)} %copy.11, f32[]{:T(128)S(6)} %sqrt.4), kind=kOutput, calls=%fused_computation.9 | convolution fusion | flops 292428992 | bytes 8126468 | tf_op jit(solution)/shard_map/ij,...jy->...iy/dot_general | solution.py:47
  113.0 4.8 %fusion.16 = f32[16,4,16,512]{3,2,1,0:T(8,128)} fusion(f32[16,4,512,16]{2,3,1,0:T(8,128)S(1)} %fusion.2, f32[]{:T(128)S(6)} %sqrt.4), kind=kOutput, calls=%fused_computation.23 | convolution fusion | flops 3223584768 | bytes 4194308 | tf_op jit(solution)/shard_map/...iy,yz->...iz/dot_general | solution.py:50
  117.8 16.3 %all-to-all-start.2 = ((f32[8,1,256]{2,1,0:T(1,128)}), f32[8,1,256]{2,1,0:T(1,128)S(1)}, u32[]{:S(2)}, u32[]{:S(2)}) async-start(f32[8,1,256]{2,1,0:T(1,128)} %bitcast.14), calls=%async_computation.2 | async-start | bytes 16384 | tf_op jit(solution)/shard_map/all_to_all | solution.py:79
  134.1 3.4 %fusion = f32[3,4,16,512]{3,2,1,0:T(8,128)S(1)} fusion(bf16[16,3,4,16,512]{4,3,2,1,0:T(8,128)(2,1)} %param.7, f32[16,4,16,512]{3,2,1,0:T(8,128)} %fusion.16), kind=kLoop, calls=%fused_computation.7 | loop fusion | flops 4620288 | bytes 5636096 | tf_op jit(solution)/shard_map/reduce_sum | solution.py:83
  137.6 11.8 %gather_fusion = f32[2048]{0:T(1024)S(1)} fusion(f32[98304]{0:T(1024)S(1)} %bitcast.57, s32[2048]{0:T(1024)S(1)} %broadcast_clamp_fusion), kind=kCustom, calls=%fused_computation | custom fusion | bytes 24576 | tf_op jit(solution)/shard_map/gather | solution.py:86
  149.4 6.6 %psum.7 = f32[8,256]{1,0:T(8,128)S(1)} all-reduce(f32[8,256]{1,0:T(8,128)S(1)} %reshape.77), channel_id=1, replica_groups=mesh['region'=8,'member'=4] {'member'}, use_global_device_ids=true, to_apply=%region_7.8 | all-reduce | flops 2048 | bytes 16384 | tf_op jit(solution)/shard_map/psum | solution.py:87
  156.0 12.0 %scatter_custom_fusion.3 = f32[98304]{0:T(1024)S(1)} fusion(s32[2048]{0:T(1024)S(1)} %bitcast.60, f32[2048]{0:T(1024)S(1)} %bitcast.64, f32[]{:T(128)} %constant.10.clone.1), kind=kCustom, calls=%fused_computation.41 | custom fusion | flops 2048 | bytes 393220 | tf_op jit(solution)/shard_map/scatter-add | solution.py:94
  168.1 2.9 %fusion.1 = f32[16,4,16,512]{3,2,1,0:T(8,128)S(1)} fusion(bf16[16,3,4,16,512]{4,3,2,1,0:T(8,128)(2,1)} %param.7, f32[3,4,16,512]{3,2,1,0:T(8,128)S(1)} %mul.50), kind=kLoop, calls=%fused_computation.8 | loop fusion | flops 4194304 | bytes 5636096 | tf_op jit(solution)/shard_map/reduce_sum | solution.py:97
  172.7 6.9 %collective-permute-start.3 = (f32[16,4,15,512]{3,0,2,1:T(8,128)S(1)}, f32[16,4,15,512]{3,0,2,1:T(8,128)S(1)}, u32[]{:S(2)}, u32[]{:S(2)}) collective-permute-start(f32[16,4,15,512]{3,0,2,1:T(8,128)S(1)} %copy.14), channel_id=1, source_target_pairs={{4,0},{8,4},{12,8},{16,12},{20,16},{24,20},{28,24},{0,28},{5,1},{9... | collective-permute-start | bytes 5898248 | tf_op jit(solution)/shard_map/ppermute | solution.py:17
  180.9 80.0 %collective-permute-done.3 = f32[16,4,15,512]{3,0,2,1:T(8,128)S(1)} collective-permute-done((f32[16,4,15,512]{3,0,2,1:T(8,128)S(1)}, f32[16,4,15,512]{3,0,2,1:T(8,128)S(1)}, u32[]{:S(2)}, u32[]{:S(2)}) %collective-permute-start.3) | collective-permute-done | bytes 1966112 | tf_op jit(solution)/shard_map/ppermute | solution.py:17
  262.0 1.2 copy.15
  263.2 6.3 %fusion.8 = f32[16,4,512,16]{2,3,1,0:T(8,128)S(1)} fusion(f32[16,4,15,512]{3,2,1,0:T(8,128)S(1)} %copy.16, f32[16,4,16,512]{3,2,1,0:T(8,128)S(1)} %fusion.1, f32[16,4,15,512]{3,2,1,0:T(8,128)S(1)} %copy.15, f32[]{:T(128)S(6)} %sqrt.4), kind=kOutput, calls=%fused_computation.15 | convolution fusion | flops 292428992 | bytes 8126468 | tf_op jit(solution)/shard_map/ij,...jy->...iy/dot_general | solution.py:47
  269.4 4.8 %fusion.18 = f32[16,4,16,512]{3,2,1,0:T(8,128)} fusion(f32[16,4,16,512]{3,2,1,0:T(8,128)S(1)} %copy-done, f32[16,4,512,16]{2,3,1,0:T(8,128)S(1)} %fusion.8, f32[]{:T(128)S(6)} %sqrt.4), kind=kOutput, calls=%fused_computation.25 | convolution fusion | flops 3224109056 | bytes 6291460 | tf_op jit(solution)/shard_map/...iy,yz->...iz/dot_general | solution.py:50
  (33 shorter events, 7.5 us)
Async XLA Ops:
  4.0 8.5 %copy-start.1 = (s32[512,1]{0,1:T(1,128)S(1)}, s32[512,1]{0,1:T(1,128)}, u32[]{:S(2)}) copy-start(s32[512,1]{0,1:T(1,128)} %param.8) | copy-start | bytes 6148
  4.0 97.2 %collective-permute-start.1 = (f32[16,4,15,512]{3,0,2,1:T(8,128)S(1)}, f32[16,4,15,512]{3,0,2,1:T(8,128)}, u32[]{:S(2)}, u32[]{:S(2)}) collective-permute-start(f32[16,4,15,512]{3,0,2,1:T(8,128)S(1)} %copy.22), channel_id=1, source_target_pairs={{4,0},{8,4},{12,8},{16,12},{20,16},{24,20},{28,24},{0,28},{5,1},{9... | collective-permute-start | bytes 5898248 | tf_op jit(solution)/shard_map/ppermute | solution.py:17
  12.4 91.5 %collective-permute-start = (f32[16,4,15,512]{3,0,2,1:T(8,128)}, f32[16,4,15,512]{3,0,2,1:T(8,128)}, u32[]{:S(2)}, u32[]{:S(2)}) collective-permute-start(f32[16,4,15,512]{3,0,2,1:T(8,128)} %copy.21), channel_id=1, source_target_pairs={{0,4},{4,8},{8,12},{12,16},{16,20},{20,24},{24,28},{28,0},{1,5},{5... | collective-permute-start | bytes 5898248 | tf_op jit(solution)/shard_map/ppermute | solution.py:16
  17.1 75.1 %all-to-all-start = ((s32[8,1,256]{2,1,0:T(1,128)}), s32[8,1,256]{2,1,0:T(1,128)S(1)}, u32[]{:S(2)}, u32[]{:S(2)}) async-start(s32[8,1,256]{2,1,0:T(1,128)} %bitcast.6), calls=%async_computation | async-start | bytes 16384 | tf_op jit(solution)/shard_map/all_to_all | solution.py:77
  92.3 25.6 %all-to-all-start.1 = ((f32[8,1,256]{2,1,0:T(1,128)}), f32[8,1,256]{2,1,0:T(1,128)S(1)}, u32[]{:S(2)}, u32[]{:S(2)}) async-start(f32[8,1,256]{2,1,0:T(1,128)} %bitcast.8), calls=%async_computation.1 | async-start | bytes 16384 | tf_op jit(solution)/shard_map/all_to_all | solution.py:80
  103.9 2.9 %copy-start = (f32[16,4,16,512]{3,2,1,0:T(8,128)S(1)}, f32[16,4,16,512]{3,2,1,0:T(8,128)}, u32[]{:S(2)}) copy-start(f32[16,4,16,512]{3,2,1,0:T(8,128)} %param.6) | copy-start | bytes 6291460
  117.8 38.2 %all-to-all-start.2 = ((f32[8,1,256]{2,1,0:T(1,128)}), f32[8,1,256]{2,1,0:T(1,128)S(1)}, u32[]{:S(2)}, u32[]{:S(2)}) async-start(f32[8,1,256]{2,1,0:T(1,128)} %bitcast.14), calls=%async_computation.2 | async-start | bytes 16384 | tf_op jit(solution)/shard_map/all_to_all | solution.py:79
  172.7 88.1 %collective-permute-start.3 = (f32[16,4,15,512]{3,0,2,1:T(8,128)S(1)}, f32[16,4,15,512]{3,0,2,1:T(8,128)S(1)}, u32[]{:S(2)}, u32[]{:S(2)}) collective-permute-start(f32[16,4,15,512]{3,0,2,1:T(8,128)S(1)} %copy.14), channel_id=1, source_target_pairs={{4,0},{8,4},{12,8},{16,12},{20,16},{24,20},{28,24},{0,28},{5,1},{9... | collective-permute-start | bytes 5898248 | tf_op jit(solution)/shard_map/ppermute | solution.py:17
  180.8 81.2 %collective-permute-start.2 = (f32[16,4,15,512]{3,0,2,1:T(8,128)S(1)}, f32[16,4,15,512]{3,0,2,1:T(8,128)S(1)}, u32[]{:S(2)}, u32[]{:S(2)}) collective-permute-start(f32[16,4,15,512]{3,0,2,1:T(8,128)S(1)} %copy.13), channel_id=1, source_target_pairs={{0,4},{4,8},{8,12},{12,16},{16,20},{20,24},{24,28},{28,0},{1,5},{5... | collective-permute-start | bytes 5898248 | tf_op jit(solution)/shard_map/ppermute | solution.py:16
where the time goes:
time: 275 us; the launch traced here: 274 us
  waiting for transfers between devices  141 us (51%)
  starting transfers between devices  44.2 us (16%)
  local copies, waits for them, and re-layouts  38.7 us (14%)
  matrix products  22.1 us (8%)
  other arithmetic  20.2 us (7%)
  blocking collectives  6.59 us (2%)
    ppermute x2, waiting for transfers between devices, extended(): after = lax.ppermute(first, axis, down)  80 us
    all_to_all x1, waiting for transfers between devices, local(): lax.all_to_all(requests, 'region', split_axis=0, concat_axis=0, tiled=True)  61.5 us
    all_to_all x1, starting transfers between devices, local(): lax.all_to_all(innov_buf, 'region', split_axis=0, concat_axis=0, tiled=True)  16.3 us
    ppermute x2, starting transfers between devices, extended(): after = lax.ppermute(first, axis, down)  13 us
    dot_general x2, matrix products, smooth(): jnp.einsum('ij,...jy->...iy', across_table, padded, precision=lax.Precisi...  12.5 us
    scatter-add x1, other arithmetic, local(): adjoint = jnp.zeros((partial_sum.size,), jnp.float32).at[flat_index].add(...  12 us
    gather x2, local copies, waits for them, and re-layouts, local(): sampled = partial_sum.reshape(-1)[index_in]  11.8 us
    dot_general x2, matrix products, smooth(): jnp.einsum('...iy,yz->...iz', across, down_table, precision=lax.Precision...  9.6 us
  transfers between devices with their start and end apart: 7, of which 2 were waited for; matrix products, arithmetic and copies ran while one was open for 18% of the time, Pallas kernels for 0%

commit v1 on v0

v1 whole, which is shorter than its diff:
```python
import functools
import math

import jax
import jax.numpy as jnp
from jax import lax
from jax.experimental import pallas as pl
from jax.experimental.pallas import tpu as pltpu
from jax.sharding import PartitionSpec as P

HALF = 15
CHUNK = 256
NORM = math.sqrt(sum(math.exp(-e * e / 36.0) for e in range(-HALF, HALF + 1)))
LIMIT = 40 * 1024 * 1024
NT_DIMS = (((1,), (1,)), ((), ()))


def band_table(count):
    step = jnp.arange(count)[None, :] - jnp.arange(count)[:, None]
    dist = step.astype(jnp.float32)
    return jnp.where(jnp.abs(step) <= HALF, jnp.exp(-dist * dist / 72.0) / NORM, 0.0)


def dot(a, b):
    return jnp.dot(a, b, preferred_element_type=jnp.float32)


def dot_nt(a, b):
    return lax.dot_general(a, b, NT_DIMS, preferred_element_type=jnp.float32)


def halves(value):
    high = value.astype(jnp.bfloat16)
    low = (value - high.astype(jnp.float32)).astype(jnp.bfloat16)
    return high, low


def filter_rows(value, table_high, table_low):
    high, low = halves(value)
    return dot(high, table_high) + (dot(high, table_low) + dot(low, table_high))


def cells_of(cell, shape):
    _, lev, width_x, width_y = shape
    y = lax.rem(cell, width_y)
    column = lax.div(cell, width_y)
    x = lax.rem(column, width_x)
    level = lax.rem(lax.div(column, width_x), lev)
    return y, column, x, level


def latitude_kernel(control_ref, high_ref, low_ref, out_high_ref, out_low_ref):
    filtered = filter_rows(control_ref[...], high_ref[...], low_ref[...])
    out_high_ref[...], out_low_ref[...] = halves(filtered)


def collect_kernel(shape, block, counts_ref, rank_ref, values_ref, members_ref, list_ref, mv_ref):
    _, _, _, width_y = shape
    group = math.prod(shape[:3])
    per_dev = members_ref.shape[0] // group
    base = pl.program_id(0) * CHUNK
    count = counts_ref[1]

    @pl.when(base >= count)
    def _():
        list_ref[...] = jnp.zeros_like(list_ref)
        mv_ref[...] = jnp.zeros_like(mv_ref)

    @pl.when(base < count)
    def _():
        slot = base + lax.broadcasted_iota(jnp.int32, (CHUNK, block), 0)

        def step(index, total):
            span = pl.ds(pl.multiple_of(index * block, block), block)
            pick = (rank_ref[:, span] == slot).astype(jnp.float32).astype(jnp.bfloat16)
            value = values_ref[:, span]
            first = value.astype(jnp.bfloat16).astype(jnp.float32)
            rest = value - first
            second = rest.astype(jnp.bfloat16).astype(jnp.float32)
            third = rest - second
            parts = jnp.concatenate([first, second, third], axis=0).astype(jnp.bfloat16)
            return total + dot_nt(parts, pick)

        start = jnp.zeros((24, CHUNK), jnp.float32)
        total = lax.fori_loop(0, rank_ref.shape[1] // block, step, start)
        found = total[0:8] + total[8:16] + total[16:24]
        list_ref[...] = found
        cell = found[0:1].astype(jnp.int32)
        y, column, _, _ = cells_of(cell, shape)
        live = base + lax.broadcasted_iota(jnp.int32, (1, CHUNK), 1) < count
        column = jnp.where(live, column, -1)
        hot = (lax.broadcasted_iota(jnp.int32, (width_y, CHUNK), 0) == y)
        hot = hot.astype(jnp.float32).astype(jnp.bfloat16)
        wanted = lax.broadcasted_iota(jnp.int32, (group, CHUNK), 0) == column
        rows = []
        for m in range(per_dev):
            here = dot(members_ref[m * group:(m + 1) * group], hot)
            rows.append(jnp.sum(jnp.where(wanted, here, 0.0), axis=0, keepdims=True))
        mv_ref[...] = jnp.concatenate(rows, axis=0).astype(jnp.bfloat16)


def footprint(shape, cell, side):
    _, lev, width_x, width_y = shape
    y, _, x, level = cells_of(cell, shape)
    hot = (lax.broadcasted_iota(jnp.int32, (width_y, CHUNK), 0) == y)
    hot = hot.astype(jnp.float32).astype(jnp.bfloat16)
    row = lax.broadcasted_iota(jnp.int32, (lev * width_x, CHUNK), 0)
    step = x + (side - 1) * width_x - lax.rem(row, width_x)
    dist = step.astype(jnp.float32)
    near = (jnp.abs(step) <= HALF) & (lax.div(row, width_x) == level)
    return hot, jnp.where(near, jnp.exp(-dist * dist / 72.0) * (1.0 / NORM), 0.0)


def sample_kernel(shape, counts_ref, list_ref, mv_ref, high_ref, low_ref, out_ref):
    side, base = pl.program_id(0), pl.program_id(1) * CHUNK
    count = counts_ref[side]
    plane = shape[1] * shape[2]
    per_dev = mv_ref.shape[1]
    group = max(1, 256 // plane)

    @pl.when(base >= count)
    def _():
        out_ref[...] = jnp.zeros_like(out_ref)

    @pl.when(base < count)
    def _():
        hot, across = footprint(shape, list_ref[0, 0:1].astype(jnp.int32), side)
        mv = mv_ref[0].astype(jnp.float32)
        total = jnp.zeros((plane, CHUNK), jnp.float32)
        for m in range(0, per_dev, group):
            rows = slice(m * plane, (m + group) * plane)
            here = dot(high_ref[rows], hot) + dot(low_ref[rows], hot)
            for k in range(group):
                total += here[k * plane:(k + 1) * plane] * mv[m + k:m + k + 1]
        out_ref[0] = jnp.sum(total * across, axis=0, keepdims=True)


def spread_kernel(
    shape, counts_ref, list_ref, mv_ref, weighted_ref, control_ref, high_ref, low_ref, out_ref, acc
):
    side, base = pl.program_id(0), pl.program_id(1) * CHUNK
    plane = shape[1] * shape[2]
    per_dev = mv_ref.shape[1]
    group = max(1, 256 // plane)

    @pl.when((side == 0) & (base == 0))
    def _():
        acc[...] = jnp.zeros_like(acc)

    @pl.when(base < counts_ref[side])
    def _():
        hot, across = footprint(shape, list_ref[0, 0:1].astype(jnp.int32), side)
        scaled = mv_ref[0].astype(jnp.float32) * weighted_ref[0]
        for m in range(0, per_dev, group):
            rows = slice(m * plane, (m + group) * plane)
            terms = [across * scaled[m + k:m + k + 1] for k in range(group)]
            high, low = halves(jnp.concatenate(terms, axis=0))
            acc[rows] += dot_nt(high, hot) + dot_nt(low, hot)

    @pl.when((side == 2) & (base + CHUNK == pl.num_programs(1) * CHUNK))
    def _():
        for r in range(0, acc.shape[0], 256):
            rows = slice(r, r + 256)
            out_ref[rows] = control_ref[rows] + filter_rows(acc[rows], high_ref[...], low_ref[...])


def local(control, members, obs_tile, obs_cell, innovation, obs_weight):
    per_dev, times, lev, width_x, width_y = members.shape
    shape = (times, lev, width_x, width_y)
    rows = per_dev * lev * width_x
    regions = lax.axis_size("region")
    me = lax.axis_index("region")
    obs_dev = obs_cell.shape[0]
    capacity = regions * (4 * obs_dev // regions)
    slots = -(-capacity // CHUNK) * CHUNK
    chunks = slots // CHUNK
    params = pltpu.CompilerParams(vmem_limit_bytes=LIMIT)
    f32, bf16 = jnp.float32, jnp.bfloat16

    packed = jnp.stack(
        [obs_cell.astype(f32), innovation, obs_weight, obs_tile[:, 0].astype(f32)]
    )
    every = lax.all_gather(packed, "region", axis=1, tiled=True)
    total = every.shape[1]

    table = band_table(width_y)
    table_high = lax.reduce_precision(table, 8, 7)
    table_low = (table - table_high).astype(bf16)
    table_high = table_high.astype(bf16)
    flat = control.reshape(rows, width_y)
    whole_table = pl.BlockSpec((width_y, width_y), lambda i: (0, 0))
    part = pl.BlockSpec((256, width_y), lambda i: (i, 0))
    field_high, field_low = pl.pallas_call(
        latitude_kernel,
        grid=(rows // 256,),
        in_specs=[part, whole_table, whole_table],
        out_specs=[part, part],
        out_shape=[jax.ShapeDtypeStruct((rows, width_y), bf16)] * 2,
        compiler_params=params,
        cost_estimate=pl.CostEstimate(
            flops=6 * rows * width_y * width_y, bytes_accessed=8 * rows * width_y, transcendentals=0
        ),
        name="latitude_filter",
    )(flat, table_high, table_low)

    owner = every[3].astype(jnp.int32)
    sides = lax.rem(me + regions + jnp.arange(-1, 2), regions)
    counts = jnp.sum((owner[None] == sides[:, None]).astype(jnp.int32), axis=1)
    mine = (owner == me).astype(f32).reshape(total // 128, 128)
    upper = (jnp.arange(128)[:, None] <= jnp.arange(128)[None, :]).astype(f32)
    inside = jnp.dot(mine, upper)
    line = jnp.arange(total // 128)
    earlier = (line[:, None] > line[None, :]).astype(f32)
    before = jnp.sum(earlier * inside[:, 127][None, :], axis=1)
    rank = jnp.where(mine > 0, (inside + before[:, None]).astype(jnp.int32) - 1, -1)
    rank = rank.reshape(1, total)
    values = jnp.concatenate([every[:3], jnp.zeros((5, total), f32)], axis=0)
    block = next(b for b in (4096, 2048, 1024, 512, 256, 128) if total % b == 0)

    listed, mv = pl.pallas_call(
        functools.partial(collect_kernel, shape, block),
        grid_spec=pltpu.PrefetchScalarGridSpec(
            num_scalar_prefetch=1,
            grid=(chunks,),
            in_specs=[
                pl.BlockSpec((1, total), lambda j, c: (0, 0)),
                pl.BlockSpec((8, total), lambda j, c: (0, 0)),
                pl.BlockSpec((per_dev * times * lev * width_x, width_y), lambda j, c: (0, 0)),
            ],
            out_specs=[
                pl.BlockSpec((8, CHUNK), lambda j, c: (0, j)),
                pl.BlockSpec((per_dev, CHUNK), lambda j, c: (0, j)),
            ],
        ),
        out_shape=[
            jax.ShapeDtypeStruct((8, slots), f32),
            jax.ShapeDtypeStruct((per_dev, slots), bf16),
        ],
        compiler_params=params,
        name="collect_members",
    )(counts, rank, values, members.reshape(-1, width_y))

    def shifted(value, by):
        pairs = [(i, (i + by) % regions) for i in range(regions)]
        return lax.ppermute(value, "region", pairs)

    short = listed[:3]
    lists = jnp.stack([shifted(short, 1), short, shifted(short, -1)])
    mvs = jnp.stack([shifted(mv, 1), mv, shifted(mv, -1)])

    list_spec = pl.BlockSpec((1, 3, CHUNK), lambda q, j, c: (q, 0, j))
    mv_spec = pl.BlockSpec((1, per_dev, CHUNK), lambda q, j, c: (q, 0, j))
    row_spec = pl.BlockSpec((1, 1, CHUNK), lambda q, j, c: (q, 0, j))
    field_spec = pl.BlockSpec((rows, width_y), lambda q, j, c: (0, 0))
    table_spec = pl.BlockSpec((width_y, width_y), lambda q, j, c: (0, 0))
    partial = pl.pallas_call(
        functools.partial(sample_kernel, shape),
        grid_spec=pltpu.PrefetchScalarGridSpec(
            num_scalar_prefetch=1,
            grid=(3, chunks),
            in_specs=[list_spec, mv_spec, field_spec, field_spec],
            out_specs=row_spec,
        ),
        out_shape=jax.ShapeDtypeStruct((3, 1, slots), f32),
        compiler_params=params,
        name="sample_increment",
    )(counts, lists, mvs, field_high, field_low)[:, 0]

    partial = lax.psum(partial, "member")
    up1 = shifted(partial[1:], 1)
    down1 = shifted(partial[:2], -1)
    up2 = shifted(partial[2], 2)
    down2 = shifted(partial[0], -2)
    modelled = partial + jnp.stack([up1[0] + up2, up1[1] + down1[0], down1[1] + down2])
    weighted = lists[:, 2] * (modelled - lists[:, 1])

    result = pl.pallas_call(
        functools.partial(spread_kernel, shape),
        grid_spec=pltpu.PrefetchScalarGridSpec(
            num_scalar_prefetch=1,
            grid=(3, chunks),
            in_specs=[
                list_spec, mv_spec, row_spec, field_spec, table_spec, table_spec,
            ],
            out_specs=field_spec,
            scratch_shapes=[pltpu.VMEM((rows, width_y), f32)],
        ),
        out_shape=jax.ShapeDtypeStruct((rows, width_y), f32),
        compiler_params=params,
        name="spread_adjoint",
    )(counts, lists, mvs, weighted[:, None], flat, table_high, table_low)
    return result.reshape(control.shape)


def solution(mesh):
    placed = (
        P("member", None, "region", None),
        P("member", None, None, "region", None),
        P("region", None),
        P("region"),
        P("region"),
        P("region"),
    )
    return jax.shard_map(
        local,
        mesh=mesh,
        in_specs=placed,
        out_specs=P("member", None, "region", None),
        check_vma=False,
    )
```

time: 275 us -> 108 us (0.39)
  waiting for transfers between devices: 141 us -> 9.1 us
  blocking collectives: 6.59 us -> 43.7 us
  local copies, waits for them, and re-layouts: 38.7 us -> 4.57 us
  matrix products: 22.1 us -> 0.13 us
  Pallas kernels: 0 us -> 19.9 us
  starting transfers between devices: 44.2 us -> 25.7 us
  other arithmetic: 20.2 us -> 3.73 us
    ppermute x4 -> x8, waiting for transfers between devices: 80 us -> 9.1 us  [shifted(): return lax.ppermute(value, 'region', pairs)]
    all_to_all x3 -> x0, waiting for transfers between devices: 61.5 us -> none  [the longest x1 61.5 us: local(): lax.all_to_all(requests, 'region', split_axis=0, concat_axis=0, tiled=True)]
    all_gather x0 -> x1, blocking collectives: none -> 32.3 us  [local(): every = lax.all_gather(packed, 'region', axis=1, tiled=True)]
    all_to_all x3 -> x0, starting transfers between devices: 31.1 us -> none  [the longest x1 16.3 us: local(): lax.all_to_all(innov_buf, 'region', split_axis=0, concat_axis=0, tiled=True)]
    dot_general x4 -> x1, matrix products: 22.1 us -> 0.13 us  [local(): inside = jnp.dot(mine, upper)]
    pallas_call x0 -> x4, Pallas kernels: none -> 19.9 us  [the longest x1 8.85 us: local(): pl.pallas_call(functools.partial(spread_kernel, shape), grid_spec=pltpu.P...]
    ppermute x4 -> x8, starting transfers between devices: 13.1 us -> 25.7 us  [shifted(): return lax.ppermute(value, 'region', pairs)]
    scatter-add x1 -> x0, other arithmetic: 12 us -> none  [local(): adjoint = jnp.zeros((partial_sum.size,), jnp.float32).at[flat_index].add(...]
  transfers between devices with their start and end apart: 7 -> 8, of which waited for: 2 -> 3; matrix products, arithmetic and copies ran while one was open for 18% -> 1% of each run, Pallas kernels for 0% -> 2%
where the time goes in v1:
time: 108 us; the launch traced here: 107 us
  blocking collectives  43.7 us (40%)
  starting transfers between devices  25.7 us (24%)
  Pallas kernels  19.9 us (18%)
  waiting for transfers between devices  9.1 us (8%)
  local copies, waits for them, and re-layouts  4.57 us (4%)
  other arithmetic  3.73 us (3%)
    all_gather x1, blocking collectives, local(): every = lax.all_gather(packed, 'region', axis=1, tiled=True)  32.3 us
    ppermute x8, starting transfers between devices, shifted(): return lax.ppermute(value, 'region', pairs)  25.7 us
    psum x1, blocking collectives, local(): partial = lax.psum(partial, 'member')  11.4 us
    ppermute x8, waiting for transfers between devices, shifted(): return lax.ppermute(value, 'region', pairs)  9.1 us
    pallas_call x1, Pallas kernels, local(): pl.pallas_call(functools.partial(spread_kernel, shape), grid_spec=pltpu.P...  8.85 us
    pallas_call x1, Pallas kernels, local(): pl.pallas_call(functools.partial(sample_kernel, shape), grid_spec=pltpu.P...  5.05 us
    pallas_call x1, Pallas kernels, local(): pl.pallas_call(functools.partial(collect_kernel, shape, block), grid_spec...  3.57 us
    unnamed x5, local copies, waits for them, and re-layouts  2.52 us
  transfers between devices with their start and end apart: 8, of which 3 were waited for; matrix products, arithmetic and copies ran while one was open for 1% of the time, Pallas kernels for 2%

profile of v1, /device:TPU:0, one launch (start us, length us, event | category | flops | bytes accessed | tf_op | source)
XLA Modules:
  0.0 107.0 jit_solution(4200169364171331653)
XLA Ops:
  0.0 0.7 convert_bitcast_fusion
  0.7 0.7 convert_element_type.54
  1.4 0.7 pad_maximum_fusion.2
  2.1 32.3 %all_gather.3 = f32[4,4096]{1,0:T(4,128)S(1)} all-gather(f32[4,512]{1,0:T(4,128)S(1)} %pad_maximum_fusion.2), channel_id=1, replica_groups=mesh['region'=8,'member'=4] {'region'}, dimensions={1}, use_global_device_ids=true | all-gather | bytes 73728 | tf_op jit(solution)/shard_map/all_gather | solution.py:183
  35.0 0.2 convert_reduce_fusion.counts_ref
  35.3 1.9 %copy-done = bf16[16,3,4,16,512]{4,3,2,1,0:T(8,128)(2,1)S(1)} copy-done((bf16[16,3,4,16,512]{4,3,2,1,0:T(8,128)(2,1)S(1)}, bf16[16,3,4,16,512]{4,3,2,1,0:T(8,128)(2,1)}, u32[]{:S(2)}) %copy-start) | copy-done | bytes 3145752
  37.1 3.6 %collect_members.1 = (f32[8,2048]{1,0:T(8,128)S(1)}, bf16[16,2048]{1,0:T(8,128)(2,1)S(1)}) custom-call(s32[3]{0:T(128)S(1)} %convert_reduce_fusion.counts_ref, s32[1,4096]{1,0:T(1,128)S(1)} %bitcast.43, f32[8,4096]{1,0:T(8,128)S(1)} %concatenate.3.values_ref, bf16[3072,512]{1,0:T(8,128)(2,1)S(1)} %bitcast.40), custom_call_target="tpu_custom_call" | custom-call | tf_op jit(solution)/shard_map/collect_members/pallas_call | solution.py:220
  40.7 4.3 %collective-permute-start.1 = (f32[3,2048]{1,0:T(4,128)S(1)}, f32[3,2048]{1,0:T(4,128)S(1)}, u32[]{:S(2)}, u32[]{:S(2)}) collective-permute-start(f32[3,2048]{1,0:T(4,128)S(1)} %get-tuple-element.14), channel_id=1, source_target_pairs={{0,28},{4,0},{8,4},{12,8},{16,12},{20,16},{24,20},{28,24},{1,29},{... | collective-permute-start | bytes 73736 | tf_op jit(solution)/shard_map/ppermute | solution.py:245
  45.0 3.0 %collective-permute-start = (f32[3,2048]{1,0:T(4,128)S(1)}, f32[3,2048]{1,0:T(4,128)S(1)}, u32[]{:S(2)}, u32[]{:S(2)}) collective-permute-start(f32[3,2048]{1,0:T(4,128)S(1)} %get-tuple-element.14), channel_id=1, source_target_pairs={{0,4},{4,8},{8,12},{12,16},{16,20},{20,24},{24,28},{28,0},{1,5},{5... | collective-permute-start | bytes 73736 | tf_op jit(solution)/shard_map/ppermute | solution.py:245
  48.0 11.6 %collective-permute-start.3 = (bf16[16,2048]{1,0:T(8,128)(2,1)S(1)}, bf16[16,2048]{1,0:T(8,128)(2,1)S(1)}, u32[]{:S(2)}, u32[]{:S(2)}) collective-permute-start(bf16[16,2048]{1,0:T(8,128)(2,1)S(1)} %get-tuple-element.10), channel_id=1, source_target_pairs={{0,28},{4,0},{8,4},{12,8},{16,12},{20,16},{24,20},{28,24},{1,29},{... | collective-permute-start | bytes 196616 | tf_op jit(solution)/shard_map/ppermute | solution.py:245
  59.8 2.4 %latitude_filter.1 = (bf16[1024,512]{1,0:T(8,128)(2,1)S(1)}, bf16[1024,512]{1,0:T(8,128)(2,1)S(1)}) custom-call(f32[1024,512]{1,0:T(8,128)S(1)} %bitcast.41, bf16[512,512]{1,0:T(8,128)(2,1)S(1)} %get-tuple-element.22.high_ref, bf16[512,512]{1,0:T(8,128)(2,1)S(1)} %get-tuple-element.23.low_ref), custom_call_target="tpu_custom_call" | custom-call | flops 1610612736 | bytes 4194304 | tf_op jit(solution)/shard_map/latitude_filter/pallas_call | solution.py:193
  62.5 4.1 %collective-permute-done.2 = bf16[16,2048]{1,0:T(8,128)(2,1)S(1)} collective-permute-done((bf16[16,2048]{1,0:T(8,128)(2,1)S(1)}, bf16[16,2048]{1,0:T(8,128)(2,1)S(1)}, u32[]{:S(2)}, u32[]{:S(2)}) %collective-permute-start.2) | collective-permute-done | bytes 65568 | tf_op jit(solution)/shard_map/ppermute | solution.py:245
  66.6 5.1 %sample_increment.1 = f32[3,1,2048]{2,1,0:T(1,128)S(1)} custom-call(s32[3]{0:T(128)S(1)} %convert_reduce_fusion.counts_ref, f32[3,3,2048]{2,1,0:T(4,128)S(1)} %copy.18.list_ref, bf16[3,16,2048]{2,1,0:T(8,128)(2,1)S(1)} %pad_maximum_fusion.mv_ref, bf16[1024,512]{1,0:T(8,128)(2,1)S(1)} %get-tuple-element.11.high_ref, ...), custom_call_target="tpu_custom_call" | custom-call | tf_op jit(solution)/shard_map/sample_increment/pallas_call | solution.py:256
  71.6 0.6 copy.21
  72.3 11.4 %psum.7 = f32[3,2048]{1,0:T(4,128)} all-reduce(f32[3,2048]{1,0:T(4,128)} %bitcast.46), channel_id=1, replica_groups=mesh['region'=8,'member'=4] {'member'}, use_global_device_ids=true, to_apply=%region_2.3 | all-reduce | flops 6144 | bytes 49152 | tf_op jit(solution)/shard_map/psum | solution.py:269
  83.7 0.8 fusion.11
  84.6 4.7 %collective-permute-start.6 = (f32[2,2048]{1,0:T(2,128)S(1)}, f32[2,2048]{1,0:T(2,128)S(1)}, u32[]{:S(2)}, u32[]{:S(2)}) collective-permute-start(f32[2,2048]{1,0:T(2,128)S(1)} %get-tuple-element.18), channel_id=1, source_target_pairs={{0,28},{4,0},{8,4},{12,8},{16,12},{20,16},{24,20},{28,24},{1,29},{... | collective-permute-start | bytes 49160 | tf_op jit(solution)/shard_map/ppermute | solution.py:245
  89.3 0.8 fusion.10
  90.1 1.7 %collective-permute-start.7 = (f32[2048]{0:T(1024)S(1)}, f32[2048]{0:T(1024)S(1)}, u32[]{:S(2)}, u32[]{:S(2)}) collective-permute-start(f32[2048]{0:T(1024)S(1)} %bitcast.56), channel_id=1, source_target_pairs={{0,24},{4,28},{8,0},{12,4},{16,8},{20,12},{24,16},{28,20},{1,25},{... | collective-permute-start | bytes 24584 | tf_op jit(solution)/shard_map/ppermute | solution.py:245
  91.8 0.4 collective-permute-start.5
  92.3 1.6 %collective-permute-done.7 = f32[2048]{0:T(1024)S(1)} collective-permute-done((f32[2048]{0:T(1024)S(1)}, f32[2048]{0:T(1024)S(1)}, u32[]{:S(2)}, u32[]{:S(2)}) %collective-permute-start.7) | collective-permute-done | bytes 8224 | tf_op jit(solution)/shard_map/ppermute | solution.py:245
  93.8 3.4 %collective-permute-done.5 = f32[2048]{0:T(1024)S(1)} collective-permute-done((f32[2048]{0:T(1024)S(1)}, f32[2048]{0:T(1024)S(1)}, u32[]{:S(2)}, u32[]{:S(2)}) %collective-permute-start.5) | collective-permute-done | bytes 8224 | tf_op jit(solution)/shard_map/ppermute | solution.py:245
  97.3 0.8 fusion.7
  98.1 8.8 %spread_adjoint.1 = f32[1024,512]{1,0:T(8,128)} custom-call(s32[3]{0:T(128)S(1)} %convert_reduce_fusion.counts_ref, f32[3,3,2048]{2,1,0:T(4,128)S(1)} %copy.18.list_ref, bf16[3,16,2048]{2,1,0:T(8,128)(2,1)S(1)} %pad_maximum_fusion.mv_ref, f32[3,1,2048]{2,1,0:T(1,128)S(1)} %broadcast_in_dim.8.weighted_ref, f32[1024,512]{1,0:T(8,128)S(1)} %bitcast.42, ...), custom_call_target="tpu_custom_call" | custom-call | tf_op jit(solution)/shard_map/spread_adjoint/pallas_call | solution.py:277
  (30 shorter events, 1.2 us)
Async XLA Ops:
  35.3 1.9 %copy-start = (bf16[16,3,4,16,512]{4,3,2,1,0:T(8,128)(2,1)S(1)}, bf16[16,3,4,16,512]{4,3,2,1,0:T(8,128)(2,1)}, u32[]{:S(2)}) copy-start(bf16[16,3,4,16,512]{4,3,2,1,0:T(8,128)(2,1)} %param.7) | copy-start | bytes 9437188
  37.1 22.7 %copy-start.1 = (f32[16,4,16,512]{3,2,1,0:T(8,128)S(1)}, f32[16,4,16,512]{3,2,1,0:T(8,128)}, u32[]{:S(2)}) copy-start(f32[16,4,16,512]{3,2,1,0:T(8,128)} %param.6) | copy-start | bytes 6291460
  40.7 21.6 %collective-permute-start.1 = (f32[3,2048]{1,0:T(4,128)S(1)}, f32[3,2048]{1,0:T(4,128)S(1)}, u32[]{:S(2)}, u32[]{:S(2)}) collective-permute-start(f32[3,2048]{1,0:T(4,128)S(1)} %get-tuple-element.14), channel_id=1, source_target_pairs={{0,28},{4,0},{8,4},{12,8},{16,12},{20,16},{24,20},{28,24},{1,29},{... | collective-permute-start | bytes 73736 | tf_op jit(solution)/shard_map/ppermute | solution.py:245
  45.0 17.3 %collective-permute-start = (f32[3,2048]{1,0:T(4,128)S(1)}, f32[3,2048]{1,0:T(4,128)S(1)}, u32[]{:S(2)}, u32[]{:S(2)}) collective-permute-start(f32[3,2048]{1,0:T(4,128)S(1)} %get-tuple-element.14), channel_id=1, source_target_pairs={{0,4},{4,8},{8,12},{12,16},{16,20},{20,24},{24,28},{28,0},{1,5},{5... | collective-permute-start | bytes 73736 | tf_op jit(solution)/shard_map/ppermute | solution.py:245
  48.0 14.5 %collective-permute-start.3 = (bf16[16,2048]{1,0:T(8,128)(2,1)S(1)}, bf16[16,2048]{1,0:T(8,128)(2,1)S(1)}, u32[]{:S(2)}, u32[]{:S(2)}) collective-permute-start(bf16[16,2048]{1,0:T(8,128)(2,1)S(1)} %get-tuple-element.10), channel_id=1, source_target_pairs={{0,28},{4,0},{8,4},{12,8},{16,12},{20,16},{24,20},{28,24},{1,29},{... | collective-permute-start | bytes 196616 | tf_op jit(solution)/shard_map/ppermute | solution.py:245
  59.6 7.0 %collective-permute-start.2 = (bf16[16,2048]{1,0:T(8,128)(2,1)S(1)}, bf16[16,2048]{1,0:T(8,128)(2,1)S(1)}, u32[]{:S(2)}, u32[]{:S(2)}) collective-permute-start(bf16[16,2048]{1,0:T(8,128)(2,1)S(1)} %get-tuple-element.10), channel_id=1, source_target_pairs={{0,4},{4,8},{8,12},{12,16},{16,20},{20,24},{24,28},{28,0},{1,5},{5... | collective-permute-start | bytes 196616 | tf_op jit(solution)/shard_map/ppermute | solution.py:245
  84.5 7.7 %collective-permute-start.4 = (f32[2,2048]{1,0:T(2,128)S(1)}, f32[2,2048]{1,0:T(2,128)S(1)}, u32[]{:S(2)}, u32[]{:S(2)}) collective-permute-start(f32[2,2048]{1,0:T(2,128)S(1)} %get-tuple-element.17), channel_id=1, source_target_pairs={{0,4},{4,8},{8,12},{12,16},{16,20},{20,24},{24,28},{28,0},{1,5},{5... | collective-permute-start | bytes 49160 | tf_op jit(solution)/shard_map/ppermute | solution.py:245
  84.6 7.6 %collective-permute-start.6 = (f32[2,2048]{1,0:T(2,128)S(1)}, f32[2,2048]{1,0:T(2,128)S(1)}, u32[]{:S(2)}, u32[]{:S(2)}) collective-permute-start(f32[2,2048]{1,0:T(2,128)S(1)} %get-tuple-element.18), channel_id=1, source_target_pairs={{0,28},{4,0},{8,4},{12,8},{16,12},{20,16},{24,20},{28,24},{1,29},{... | collective-permute-start | bytes 49160 | tf_op jit(solution)/shard_map/ppermute | solution.py:245
  90.1 3.7 %collective-permute-start.7 = (f32[2048]{0:T(1024)S(1)}, f32[2048]{0:T(1024)S(1)}, u32[]{:S(2)}, u32[]{:S(2)}) collective-permute-start(f32[2048]{0:T(1024)S(1)} %bitcast.56), channel_id=1, source_target_pairs={{0,24},{4,28},{8,0},{12,4},{16,8},{20,12},{24,16},{28,20},{1,25},{... | collective-permute-start | bytes 24584 | tf_op jit(solution)/shard_map/ppermute | solution.py:245
  91.8 5.4 %collective-permute-start.5 = (f32[2048]{0:T(1024)S(1)}, f32[2048]{0:T(1024)S(1)}, u32[]{:S(2)}, u32[]{:S(2)}) collective-permute-start(f32[2048]{0:T(1024)S(1)} %bitcast.55), channel_id=1, source_target_pairs={{0,8},{4,12},{8,16},{12,20},{16,24},{20,28},{24,0},{28,4},{1,9},{5... | collective-permute-start | bytes 24584 | tf_op jit(solution)/shard_map/ppermute | solution.py:245
